TPU v7x, 32 devices: a whole 2x2x4 slice. The times are simulated.
32 devices in a mesh: grp: 2 (over y), exp: 16 (over z, x, core).
Axes of the slice: x: 2, y: 2, z: 4, core: 2. Of those that a mesh axis runs over, the one named last changes fastest.
Arguments:
- tokens: bfloat16 [4096, 1024], P(('grp', 'exp')), may hold values from -6 to 6
- w_in: bfloat16 [32, 1024, 768], P('exp', 'grp'), may hold values from -0.1875 to 0.1875
- w_out: bfloat16 [32, 384, 1024], P('exp', 'grp'), may hold values from -0.3125 to 0.3125
- moments_in: bfloat16 [32, 2, 1024, 768], P('exp', None, 'grp'), may hold values from -6 to 6
- moments_out: bfloat16 [32, 2, 384, 1024], P('exp', None, 'grp'), may hold values from -6 to 6
- expert_ids: int32 [4096, 8], P(('grp', 'exp')), may hold values from 0 to 23, all different within a row; in each aligned block of 128 rows (0 to 127, 128 to 255, ...) at most 64 rows name the same one
- route_weights: float32 [4096, 8], P(('grp', 'exp')), may hold values from 0.1 to 1
- old_plan: int32 [32], replicated, may hold values from 0 to 23, as said below
- new_plan: int32 [32], replicated, may hold values from 0 to 23, as said below
Outputs:
- mixed: bfloat16 [4096, 1024], P(('grp', 'exp'))
- new_w_in: bfloat16 [32, 1024, 768], P('exp', 'grp')
- new_w_out: bfloat16 [32, 384, 1024], P('exp', 'grp')
- new_moments_in: bfloat16 [32, 2, 1024, 768], P('exp', None, 'grp')
- new_moments_out: bfloat16 [32, 2, 384, 1024], P('exp', None, 'grp')
Inputs may be any that keep to these rules, and one draw needn't show every extreme that they name: `expert_ids`: each row names 8 different experts. Among the rows of one device no expert is named more than 64 times, and in every draw some device names some expert exactly 64 times. `old_plan`: every expert is held by one or two slots; exactly 8 experts are held by two. `new_plan`: every expert is held by one or two slots; exactly 8 experts are held by two.
All inputs are finite; a program needn't handle non-finite values.
Results may differ from a plain program's by a relative error of at most 0.0057.
Values may be sent and summed in bfloat16 or wider, within the bound.
No kernel may reach another device: no remote copies, remote signals or barrier semaphores. Data moves between devices by JAX's collectives and lax.ppermute only.
A program may use at most 64 MiB of HBM per device.

v0:
```python
import jax
import jax.numpy as jnp
from jax import lax
from jax.sharding import PartitionSpec as P

TOP = 8
TOK_DEV = 128


def on_device(
    tokens, w_in, w_out, moments_in, moments_out, expert_ids, route_weights, old_plan, new_plan
):
    device_count = lax.axis_size("exp")
    per_device = w_in.shape[0]
    slot_count = per_device * device_count
    expert_count = 3 * device_count // 2
    capacity = 3 * TOK_DEV * TOP // (2 * expert_count)
    width = tokens.shape[1]
    token_count = tokens.shape[0]
    slot_index = jnp.arange(slot_count, dtype=jnp.int32)
    same_expert = new_plan[:, None] == old_plan[None, :]
    source = jnp.min(jnp.where(same_expert, slot_index[None, :], slot_count), axis=1)
    flat_in = w_in.reshape(per_device, -1)
    flat_out = w_out.reshape(per_device, -1)
    flat_moments_in = moments_in.reshape(per_device, -1)
    flat_moments_out = moments_out.reshape(per_device, -1)
    spread = (
        lax.all_to_all(flat_in, "exp", split_axis=1, concat_axis=0, tiled=True),
        lax.all_to_all(flat_out, "exp", split_axis=1, concat_axis=0, tiled=True),
        lax.all_to_all(flat_moments_in, "exp", split_axis=1, concat_axis=0, tiled=True),
        lax.all_to_all(flat_moments_out, "exp", split_axis=1, concat_axis=0, tiled=True),
    )
    picked = tuple((jnp.take(piece, source, axis=0) for piece in spread))
    landed = (
        lax.all_to_all(picked[0], "exp", split_axis=0, concat_axis=1, tiled=True),
        lax.all_to_all(picked[1], "exp", split_axis=0, concat_axis=1, tiled=True),
        lax.all_to_all(picked[2], "exp", split_axis=0, concat_axis=1, tiled=True),
        lax.all_to_all(picked[3], "exp", split_axis=0, concat_axis=1, tiled=True),
    )
    new_w_in = landed[0].reshape(w_in.shape)
    new_w_out = landed[1].reshape(w_out.shape)
    new_moments_in = landed[2].reshape(moments_in.shape)
    new_moments_out = landed[3].reshape(moments_out.shape)
    full_in, full_out = (
        lax.all_gather(w_in, "grp", axis=1, tiled=True),
        lax.all_gather(w_out, "grp", axis=1, tiled=True),
    )
    hidden_size = full_out.shape[1]
    pair_count = token_count * TOP
    pair_expert = expert_ids.reshape(-1)
    expert_index = jnp.arange(expert_count, dtype=jnp.int32)
    holders = old_plan[None, :] == expert_index[:, None]
    first_slot = jnp.min(jnp.where(holders, slot_index[None, :], slot_count), axis=1)
    chosen = pair_expert[:, None] == expert_index[None, :]
    pair_first = jnp.sum(jnp.where(chosen, first_slot[None, :], 0), axis=1)
    onehot = (pair_first[:, None] == slot_index[None, :]).astype(jnp.int32)
    running = jnp.cumsum(onehot, axis=0)
    position = jnp.sum(onehot * running, axis=1) - 1
    target = pair_first * capacity + position
    pair_token = jnp.arange(pair_count, dtype=jnp.int32) // TOP
    outgoing = (
        jnp.zeros((slot_count * capacity, width), jnp.bfloat16).at[target].set(tokens[pair_token])
    )
    outgoing = outgoing.reshape(device_count, per_device, capacity, width)
    both = jnp.einsum(
        "njcd,jdh->njch",
        lax.all_to_all(outgoing, "exp", split_axis=0, concat_axis=0, tiled=True),
        full_in,
        preferred_element_type=jnp.float32,
    )
    hidden = (jax.nn.silu(both[..., :hidden_size]) * both[..., hidden_size:]).astype(jnp.bfloat16)
    result = jnp.einsum(
        "njch,jhd->njcd", hidden, full_out, preferred_element_type=jnp.float32
    ).astype(jnp.bfloat16)
    returned = lax.all_to_all(result, "exp", split_axis=0, concat_axis=0, tiled=True)
    returned = returned.reshape(slot_count * capacity, width)
    gathered = jnp.take(returned, target, axis=0).reshape(token_count, TOP, width)
    share = route_weights / jnp.sum(route_weights, axis=1, keepdims=True)
    mixed = jnp.sum(share[:, :, None] * gathered.astype(jnp.float32), axis=1).astype(jnp.bfloat16)
    return (mixed, new_w_in, new_w_out, new_moments_in, new_moments_out)


def solution(mesh):
    return jax.shard_map(
        on_device,
        mesh=mesh,
        in_specs=(
            P(("grp", "exp"), None),
            P("exp", "grp", None),
            P("exp", "grp", None),
            P("exp", None, "grp", None),
            P("exp", None, "grp", None),
            P(("grp", "exp"), None),
            P(("grp", "exp"), None),
            P(),
            P(),
        ),
        out_specs=(
            P(("grp", "exp"), None),
            P("exp", "grp", None),
            P("exp", "grp", None),
            P("exp", None, "grp", None),
            P("exp", None, "grp", None),
        ),
        check_vma=False,
    )
```

profile of v0, /device:TPU:11, one launch (start us, length us, event | category | flops | bytes accessed | tf_op | source)
XLA Modules:
  0.0 619.6 jit_solution(9765553671902233325)
XLA Ops:
  7.2 2.4 all_to_all.115
  11.3 6.6 %all-to-all-start.4 = ((bf16[2,16,12288]{2,0,1:T(2,128)(2,1)}), bf16[2,16,12288]{2,0,1:T(2,128)(2,1)}, u32[]{:S(2)}, u32[]{:S(2)}) async-start(bf16[2,16,12288]{2,0,1:T(2,128)(2,1)} %copy.59), calls=%async_computation.4 | async-start | bytes 1572864 | tf_op jit(solution)/shard_map/all_to_all | solution.py:29
  18.6 2.8 copy.57
  21.4 15.8 %all-to-all-done.4 = bf16[2,16,12288]{2,0,1:T(2,128)(2,1)} async-done(((bf16[2,16,12288]{2,0,1:T(2,128)(2,1)}), bf16[2,16,12288]{2,0,1:T(2,128)(2,1)}, u32[]{:S(2)}, u32[]{:S(2)}) %all-to-all-start.4) | async-done | bytes 786464 | tf_op jit(solution)/shard_map/all_to_all | solution.py:29
  37.2 5.0 all-to-all-start.2
  44.0 2.8 copy.63
  47.2 31.1 %all-to-all-done.2 = bf16[2,16,24576]{2,0,1:T(2,128)(2,1)S(1)} async-done(((bf16[2,16,24576]{2,0,1:T(2,128)(2,1)}), bf16[2,16,24576]{2,0,1:T(2,128)(2,1)S(1)}, u32[]{:S(2)}, u32[]{:S(2)}) %all-to-all-start.2) | async-done | bytes 1572896 | tf_op jit(solution)/shard_map/all_to_all | solution.py:28
  78.3 4.9 all-to-all-start.8
  83.2 2.3 all_to_all.118
  89.4 30.1 %all-to-all-done.8 = bf16[2,16,24576]{2,0,1:T(2,128)(2,1)} async-done(((bf16[2,16,24576]{2,0,1:T(2,128)(2,1)}), bf16[2,16,24576]{2,0,1:T(2,128)(2,1)}, u32[]{:S(2)}, u32[]{:S(2)}) %all-to-all-start.8) | async-done | bytes 1572896 | tf_op jit(solution)/shard_map/all_to_all | solution.py:31
  119.5 5.5 all-to-all-start.5
  126.8 2.7 gather_fusion.3
  129.5 2.7 gather_fusion.4
  132.2 3.4 broadcast_select_fusion.1
  137.5 6.8 %all-to-all-done.5 = bf16[16,2,12288]{2,1,0:T(2,128)(2,1)} async-done(((bf16[16,2,12288]{2,1,0:T(2,128)(2,1)}), bf16[16,2,12288]{2,1,0:T(2,128)(2,1)}, u32[]{:S(2)}, u32[]{:S(2)}) %all-to-all-start.5) | async-done | bytes 786464 | tf_op jit(solution)/shard_map/all_to_all | solution.py:36
  144.2 4.9 all-to-all-start.3
  149.2 3.4 all_to_all.121
  152.6 4.9 copy.61
  157.5 27.9 %all-to-all-done.3 = bf16[16,2,24576]{2,1,0:T(2,128)(2,1)} async-done(((bf16[16,2,24576]{2,1,0:T(2,128)(2,1)}), bf16[16,2,24576]{2,1,0:T(2,128)(2,1)}, u32[]{:S(2)}, u32[]{:S(2)}) %all-to-all-start.3) | async-done | bytes 1572896 | tf_op jit(solution)/shard_map/all_to_all | solution.py:35
  185.5 4.9 all-to-all-start.6
  190.4 3.0 all_to_all.131
  193.4 66.9 %all-to-all-done.6 = bf16[2,16,49152]{2,0,1:T(2,128)(2,1)S(1)} async-done(((bf16[2,16,49152]{2,0,1:T(2,128)(2,1)}), bf16[2,16,49152]{2,0,1:T(2,128)(2,1)S(1)}, u32[]{:S(2)}, u32[]{:S(2)}) %all-to-all-start.6) | async-done | bytes 3145760 | tf_op jit(solution)/shard_map/all_to_all | solution.py:30
  260.3 5.2 all-to-all-start.9
  267.2 15.7 %reduce-window.6 = s32[32,8,128]{2,1,0:T(8,128)S(1)} reduce-window(s32[32,8,128]{2,1,0:T(8,128)} %fusion.17, s32[]{:T(128)} %constant.79.clone.1), window={size=1x1x128 pad=0_0x0_0x127_0}, to_apply=%region_3.4 | reduce-window | flops 4161536 | bytes 262148 | tf_op jit(solution)/shard_map/reduce-window
  287.6 15.3 %scatter_custom_fusion = bf16[2048,1024]{1,0:T(8,128)(2,1)} fusion(s32[1024]{0:T(1024)S(1)} %bitcast.64, bf16[128,1024]{1,0:T(8,128)(2,1)S(1)} %copy-done, s32[1024]{0:T(1024)S(1)} %broadcast_clamp_fusion.1, bf16[]{:T(256)} %constant.84.clone.1), kind=kCustom, calls=%fused_computation.17 | custom fusion | bytes 4194306 | tf_op jit(solution)/shard_map/scatter | solution.py:62
  302.9 3.3 all_to_all.124
  306.2 4.4 gather_fusion.2
  310.6 3.8 gather.30
  314.4 6.4 %all-to-all-start = ((bf16[16,2,64,1024]{3,2,1,0:T(8,128)(2,1)}), bf16[16,2,64,1024]{3,2,1,0:T(8,128)(2,1)}, u32[]{:S(2)}, u32[]{:S(2)}) async-start(bf16[16,2,64,1024]{3,2,1,0:T(8,128)(2,1)} %bitcast.56), calls=%async_computation | async-start | bytes 8388608 | tf_op jit(solution)/shard_map/all_to_all | solution.py:67
  320.8 4.4 broadcast_select_fusion
  325.3 87.9 %all-to-all-done = bf16[16,2,64,1024]{3,2,1,0:T(8,128)(2,1)} async-done(((bf16[16,2,64,1024]{3,2,1,0:T(8,128)(2,1)}), bf16[16,2,64,1024]{3,2,1,0:T(8,128)(2,1)}, u32[]{:S(2)}, u32[]{:S(2)}) %all-to-all-start) | async-done | bytes 4194336 | tf_op jit(solution)/shard_map/all_to_all | solution.py:67
  413.1 4.9 all-to-all-start.7
  419.5 46.5 %all-gather.3.cloned.1.call-done = bf16[2,1024,768]{2,1,0:T(8,128)(2,1)} async-done(((bf16[2,512,768]{2,1,0:T(8,128)(2,1)}), bf16[2,1024,768]{2,1,0:T(8,128)(2,1)}) %all-gather.3.cloned.1.call-update) | async-done | bytes 3145744 | tf_op jit(solution)/shard_map/all_gather | solution.py:45
  466.0 9.2 %fusion.4 = f32[16,2,64,768]{3,2,0,1:T(8,128)} fusion(bf16[2,1024,768]{2,1,0:T(8,128)(2,1)} %all-gather.3.cloned.1.call-done, bf16[16,2,64,1024]{3,2,1,0:T(8,128)(2,1)} %all-to-all-done), kind=kOutput, calls=%fused_computation.15 | convolution fusion | flops 3221225472 | bytes 13631488 | tf_op jit(solution)/shard_map/njcd,jdh->njch/dot_general | solution.py:65
  475.2 19.6 %all-gather.5.cloned.1.call-done = bf16[2,384,1024]{2,1,0:T(8,128)(2,1)} async-done(((bf16[2,192,1024]{2,1,0:T(8,128)(2,1)}), bf16[2,384,1024]{2,1,0:T(8,128)(2,1)}) %all-gather.5.cloned.1.call-update) | async-done | bytes 1572880 | tf_op jit(solution)/shard_map/all_gather | solution.py:46
  494.8 5.6 convert_bitcast_fusion
  500.4 2.7 copy.56
  503.1 6.9 %all-to-all-start.1 = ((bf16[16,2,64,1024]{3,2,1,0:T(8,128)(2,1)}), bf16[16,2,64,1024]{3,2,1,0:T(8,128)(2,1)}, u32[]{:S(2)}, u32[]{:S(2)}) async-start(bf16[16,2,64,1024]{3,2,1,0:T(8,128)(2,1)} %copy.56), calls=%async_computation.1 | async-start | bytes 8388608 | tf_op jit(solution)/shard_map/all_to_all | solution.py:75
  510.3 2.4 copy.60
  512.7 3.0 reshape.217
  515.7 3.4 copy.58
  519.1 2.7 reshape.216
  521.9 3.4 copy.64
  525.3 2.7 reshape.219
  528.0 3.4 copy.62
  531.4 4.8 reshape.218
  536.2 66.1 %all-to-all-done.1 = bf16[16,2,64,1024]{3,2,1,0:T(8,128)(2,1)} async-done(((bf16[16,2,64,1024]{3,2,1,0:T(8,128)(2,1)}), bf16[16,2,64,1024]{3,2,1,0:T(8,128)(2,1)}, u32[]{:S(2)}, u32[]{:S(2)}) %all-to-all-start.1) | async-done | bytes 4194336 | tf_op jit(solution)/shard_map/all_to_all | solution.py:75
  602.3 7.7 %gather_fusion = bf16[1024,1024]{1,0:T(8,128)(2,1)S(1)} fusion(bf16[2048,1024]{1,0:T(8,128)(2,1)} %bitcast.13, s32[1024]{0:T(1024)S(1)} %broadcast_clamp_fusion), kind=kCustom, calls=%fused_computation.3 | custom fusion | bytes 4198400 | tf_op jit(solution)/shard_map/jit(_take)/gather | solution.py:77
  (70 shorter events, 22.4 us)
Async XLA Ops:
  7.2 280.4 %copy-start = (bf16[128,1024]{1,0:T(8,128)(2,1)S(1)}, bf16[128,1024]{1,0:T(8,128)(2,1)}, u32[]{:S(2)}) copy-start(bf16[128,1024]{1,0:T(8,128)(2,1)} %param.11) | copy-start | bytes 786436
  7.2 10.7 %copy-start.3 = (bf16[2,512,768]{2,1,0:T(8,128)(2,1)S(1)}, bf16[2,512,768]{2,1,0:T(8,128)(2,1)}, u32[]{:S(2)}) copy-start(bf16[2,512,768]{2,1,0:T(8,128)(2,1)} %param.12) | copy-start | bytes 4718596
  11.3 25.9 %all-to-all-start.4 = ((bf16[2,16,12288]{2,0,1:T(2,128)(2,1)}), bf16[2,16,12288]{2,0,1:T(2,128)(2,1)}, u32[]{:S(2)}, u32[]{:S(2)}) async-start(bf16[2,16,12288]{2,0,1:T(2,128)(2,1)} %copy.59), calls=%async_computation.4 | async-start | bytes 1572864 | tf_op jit(solution)/shard_map/all_to_all | solution.py:29
  37.2 41.1 %all-to-all-start.2 = ((bf16[2,16,24576]{2,0,1:T(2,128)(2,1)}), bf16[2,16,24576]{2,0,1:T(2,128)(2,1)S(1)}, u32[]{:S(2)}, u32[]{:S(2)}) async-start(bf16[2,16,24576]{2,0,1:T(2,128)(2,1)} %copy.57), calls=%async_computation.2 | async-start | bytes 3145728 | tf_op jit(solution)/shard_map/all_to_all | solution.py:28
  42.1 4.7 copy-start.10
  42.1 4.7 copy-start.11
  47.1 39.4 %copy-start.8 = (s32[1024]{0:T(1024)}, s32[1024]{0:T(1024)S(1)}, u32[]{:S(2)}) copy-start(s32[1024]{0:T(1024)S(1)} %pad_clamp_fusion) | copy-start | bytes 12292
  47.2 39.9 %copy-start.5 = (pred[16,2]{1,0:T(8,128)(4,1)}, pred[16,2]{1,0:T(8,128)(4,1)S(1)}, u32[]{:S(2)}) copy-start(pred[16,2]{1,0:T(8,128)(4,1)S(1)} %compare_and_fusion.1) | copy-start | bytes 100
  78.3 41.2 %all-to-all-start.8 = ((bf16[2,16,24576]{2,0,1:T(2,128)(2,1)}), bf16[2,16,24576]{2,0,1:T(2,128)(2,1)}, u32[]{:S(2)}, u32[]{:S(2)}) async-start(bf16[2,16,24576]{2,0,1:T(2,128)(2,1)} %copy.63), calls=%async_computation.8 | async-start | bytes 3145728 | tf_op jit(solution)/shard_map/all_to_all | solution.py:31
  119.5 24.7 %all-to-all-start.5 = ((bf16[16,2,12288]{2,1,0:T(2,128)(2,1)}), bf16[16,2,12288]{2,1,0:T(2,128)(2,1)}, u32[]{:S(2)}, u32[]{:S(2)}) async-start(bf16[16,2,12288]{2,1,0:T(2,128)(2,1)} %broadcast_select_fusion.3), calls=%async_computation.5 | async-start | bytes 1572864 | tf_op jit(solution)/shard_map/all_to_all | solution.py:36
  144.2 41.2 %all-to-all-start.3 = ((bf16[16,2,24576]{2,1,0:T(2,128)(2,1)}), bf16[16,2,24576]{2,1,0:T(2,128)(2,1)}, u32[]{:S(2)}, u32[]{:S(2)}) async-start(bf16[16,2,24576]{2,1,0:T(2,128)(2,1)} %all_to_all.112), calls=%async_computation.3 | async-start | bytes 3145728 | tf_op jit(solution)/shard_map/all_to_all | solution.py:35
  185.5 74.8 %all-to-all-start.6 = ((bf16[2,16,49152]{2,0,1:T(2,128)(2,1)}), bf16[2,16,49152]{2,0,1:T(2,128)(2,1)S(1)}, u32[]{:S(2)}, u32[]{:S(2)}) async-start(bf16[2,16,49152]{2,0,1:T(2,128)(2,1)} %copy.61), calls=%async_computation.6 | async-start | bytes 6291456 | tf_op jit(solution)/shard_map/all_to_all | solution.py:30
  190.4 75.1 %copy-start.9 = (s32[128,8]{0,1:T(8,128)S(1)}, s32[128,8]{0,1:T(8,128)}, u32[]{:S(2)}) copy-start(s32[128,8]{0,1:T(8,128)} %param.16) | copy-start | bytes 12292
  260.3 42.6 %copy-start.2 = (bf16[2,16,49152]{2,0,1:T(2,128)(2,1)}, bf16[2,16,49152]{2,0,1:T(2,128)(2,1)S(1)}, u32[]{:S(2)}) copy-start(bf16[2,16,49152]{2,0,1:T(2,128)(2,1)S(1)} %all-to-all-done.6) | copy-start | bytes 9437188
  260.3 54.2 %all-to-all-start.9 = ((bf16[16,2,24576]{2,1,0:T(2,128)(2,1)}), bf16[16,2,24576]{2,1,0:T(2,128)(2,1)}, u32[]{:S(2)}, u32[]{:S(2)}) async-start(bf16[16,2,24576]{2,1,0:T(2,128)(2,1)} %all_to_all.131), calls=%async_computation.9 | async-start | bytes 3145728 | tf_op jit(solution)/shard_map/all_to_all | solution.py:38
  265.9 0.6 copy-start.4
  314.4 6.4 %copy-start.6 = (pred[16,2]{1,0:T(8,128)(4,1)S(1)}, pred[16,2]{1,0:T(8,128)(4,1)}, u32[]{:S(2)}) copy-start(pred[16,2]{1,0:T(8,128)(4,1)} %copy-done.5) | copy-start | bytes 100
  314.4 98.7 %all-to-all-start = ((bf16[16,2,64,1024]{3,2,1,0:T(8,128)(2,1)}), bf16[16,2,64,1024]{3,2,1,0:T(8,128)(2,1)}, u32[]{:S(2)}, u32[]{:S(2)}) async-start(bf16[16,2,64,1024]{3,2,1,0:T(8,128)(2,1)} %bitcast.56), calls=%async_computation | async-start | bytes 8388608 | tf_op jit(solution)/shard_map/all_to_all | solution.py:67
  413.1 89.9 %all-to-all-start.7 = ((bf16[16,2,49152]{2,1,0:T(2,128)(2,1)}), bf16[16,2,49152]{2,1,0:T(2,128)(2,1)S(1)}, u32[]{:S(2)}, u32[]{:S(2)}) async-start(bf16[16,2,49152]{2,1,0:T(2,128)(2,1)} %broadcast_select_fusion), calls=%async_computation.7 | async-start | bytes 6291456 | tf_op jit(solution)/shard_map/all_to_all | solution.py:37
  418.0 47.9 %all-gather.3.cloned.1.call-start = ((), (), s32[]{:S(2)}) async-start(), calls=%async_computation.10 | async-start | bytes 4718592 | tf_op jit(solution)/shard_map/all_gather | solution.py:45
  418.8 76.0 %all-gather.5.cloned.1.call-start = ((), (), s32[]{:S(2)}) async-start(), calls=%async_computation.11 | async-start | bytes 2359296 | tf_op jit(solution)/shard_map/all_gather | solution.py:46
  503.1 7.0 %copy-start.7 = (f32[128,8]{0,1:T(8,128)S(1)}, f32[128,8]{0,1:T(8,128)}, u32[]{:S(2)}) copy-start(f32[128,8]{0,1:T(8,128)} %param.17) | copy-start | bytes 12292
  503.1 99.2 %all-to-all-start.1 = ((bf16[16,2,64,1024]{3,2,1,0:T(8,128)(2,1)}), bf16[16,2,64,1024]{3,2,1,0:T(8,128)(2,1)}, u32[]{:S(2)}, u32[]{:S(2)}) async-start(bf16[16,2,64,1024]{3,2,1,0:T(8,128)(2,1)} %copy.56), calls=%async_computation.1 | async-start | bytes 8388608 | tf_op jit(solution)/shard_map/all_to_all | solution.py:75
  602.3 10.0 %copy-start.1 = (bf16[128,1024]{1,0:T(8,128)(2,1)S(1)}, bf16[128,1024]{1,0:T(8,128)(2,1)}, u32[]{:S(2)}) copy-start(bf16[128,1024]{1,0:T(8,128)(2,1)} %param.11) | copy-start | bytes 786436
Sparse Core Ops, SparseCore 0:
  420.4 45.5 all-gather.2
  467.5 27.2 all-gather.4
where the time goes:
time: 629 us; the launch traced here: 620 us
  waiting for transfers between devices  400 us (64%)
  local copies, waits for them, and re-layouts  105 us (17%)
  starting transfers between devices  55.3 us (9%)
  other arithmetic  30.1 us (5%)
  between operations  14.9 us (2%)
  matrix products  14.8 us (2%)
    all_to_all x1, waiting for transfers between devices, on_device(): lax.all_to_all(outgoing, 'exp', split_axis=0, concat_axis=0, tiled=True)  87.9 us
    all_to_all x1, waiting for transfers between devices, on_device(): lax.all_to_all(flat_moments_in, 'exp', split_axis=1, concat_axis=0, tiled...  66.9 us
    all_to_all x1, waiting for transfers between devices, on_device(): lax.all_to_all(result, 'exp', split_axis=0, concat_axis=0, tiled=True)  66.1 us
    all_gather x1, waiting for transfers between devices, on_device(): lax.all_gather(w_in, 'grp', axis=1, tiled=True)  46.5 us
    all_to_all x1, waiting for transfers between devices, on_device(): lax.all_to_all(flat_in, 'exp', split_axis=1, concat_axis=0, tiled=True)  31.1 us
    all_to_all x1, waiting for transfers between devices, on_device(): lax.all_to_all(flat_moments_out, 'exp', split_axis=1, concat_axis=0, tile...  30.1 us
    all_to_all x1, waiting for transfers between devices, on_device(): lax.all_to_all(picked[0], 'exp', split_axis=0, concat_axis=1, tiled=True)  27.9 us
    all_gather x1, waiting for transfers between devices, on_device(): lax.all_gather(w_out, 'grp', axis=1, tiled=True)  19.6 us
  transfers between devices with their start and end apart: 12, of which 10 were waited for; matrix products, arithmetic and copies ran while one was open for 19% of the time, Pallas kernels for 0%

commit v1 on v0

v1 whole, which is shorter than its diff:
```python
import jax
import jax.numpy as jnp
from jax import lax
from jax.experimental import pallas as pl
from jax.experimental.pallas import tpu as pltpu
from jax.sharding import PartitionSpec as P

SUB = 8
LANE = 128
PARTIAL_BYTES = 8 * 1024 * 1024


def to_tiles(x):
    slots, columns = x.shape[0], x.shape[-1]
    x = x.reshape(slots, -1, SUB, columns // LANE, LANE)
    return x.swapaxes(2, 3).reshape(slots, -1, SUB, LANE)


def from_tiles(x, shape):
    columns = shape[-1]
    x = x.reshape(shape[0], -1, columns // LANE, SUB, LANE)
    return x.swapaxes(2, 3).reshape(shape)


def reshuffle(arrays, source, devices):
    tiles = [to_tiles(a) for a in arrays]
    counts = [t.shape[1] for t in tiles]
    total = sum(counts)
    extra = -total % devices
    if extra:
        tiles.append(jnp.zeros((tiles[0].shape[0], extra, SUB, LANE), tiles[0].dtype))
    packed = jnp.concatenate(tiles, axis=1) if len(tiles) > 1 else tiles[0]
    slots = packed.shape[0]
    part = packed.shape[1] // devices
    packed = packed.reshape(slots, devices, part, SUB, LANE).swapaxes(0, 1)
    spread = lax.all_to_all(packed, "exp", split_axis=0, concat_axis=0, tiled=True)
    spread = spread.reshape(devices * slots, part, SUB, LANE)
    picked = jnp.take(spread, source, axis=0, mode="clip")
    picked = picked.reshape(devices, slots, part, SUB, LANE)
    landed = lax.all_to_all(picked, "exp", split_axis=0, concat_axis=0, tiled=True)
    landed = landed.swapaxes(0, 1).reshape(slots, devices * part, SUB, LANE)
    outs, at = [], 0
    for a, count in zip(arrays, counts):
        outs.append(from_tiles(landed[:, at : at + count], a.shape))
        at += count
    return outs


def expert_kernel(first_ref, x_ref, w_in_ref, w_out_ref, out_ref):
    slots, width, _ = w_in_ref.shape
    hidden_size = w_out_ref.shape[1]
    half = (x_ref.shape[1] - width) // 2
    x = x_ref[:, :width]
    weights = x_ref[:, width:].astype(jnp.float32)
    lane = lax.broadcasted_iota(jnp.int32, weights.shape, 1)
    total = jnp.zeros(out_ref.shape, jnp.float32)
    for j in range(slots):
        both = jnp.dot(x, w_in_ref[j], preferred_element_type=jnp.float32)
        gate, up = both[:, :hidden_size], both[:, hidden_size:]
        hidden = (gate / (1.0 + jnp.exp(-gate)) * up).astype(jnp.bfloat16)
        result = jnp.dot(hidden, w_out_ref[j], preferred_element_type=jnp.float32)
        result = result.astype(jnp.bfloat16).astype(jnp.float32)
        at = first_ref[0] + j
        mine = (lane == at) | (lane == at + half)
        weight = jnp.sum(jnp.where(mine, weights, 0.0), axis=1, keepdims=True)
        total = total + weight * result
    out_ref[...] = total.astype(out_ref.dtype)


def experts(x, w_in, w_out, first):
    rows, columns = x.shape
    slots, width, hidden2 = w_in.shape
    block = 256 if rows % 256 == 0 else rows
    return pl.pallas_call(
        expert_kernel,
        grid=(rows // block,),
        in_specs=[
            pl.BlockSpec(memory_space=pltpu.SMEM),
            pl.BlockSpec((block, columns), lambda i: (i, 0)),
            pl.BlockSpec(w_in.shape, lambda i: (0, 0, 0)),
            pl.BlockSpec(w_out.shape, lambda i: (0, 0, 0)),
        ],
        out_specs=pl.BlockSpec((block, width), lambda i: (i, 0)),
        out_shape=jax.ShapeDtypeStruct((rows, width), jnp.float32),
        compiler_params=pltpu.CompilerParams(vmem_limit_bytes=40 * 1024 * 1024),
        cost_estimate=pl.CostEstimate(
            flops=3 * rows * slots * width * hidden2,
            bytes_accessed=rows * columns * 2 + rows * width * 4 + w_in.size * 3,
            transcendentals=rows * slots * hidden2 // 2,
        ),
    )(first, x, w_in, w_out)


def on_device(
    tokens, w_in, w_out, moments_in, moments_out, expert_ids, route_weights, old_plan, new_plan
):
    devices = lax.axis_size("exp")
    per_device = w_in.shape[0]
    slot_count = per_device * devices
    slot_index = jnp.arange(slot_count, dtype=jnp.int32)

    share = route_weights / jnp.sum(route_weights, axis=1, keepdims=True)
    earlier = (old_plan[None, :] == old_plan[:, None]) & (slot_index[None, :] < slot_index[:, None])
    is_first = ~jnp.any(earlier, axis=1)
    chosen = (expert_ids[:, :, None] == old_plan[None, None, :]) & is_first[None, None, :]
    weight = jnp.sum(jnp.where(chosen, share[:, :, None], 0.0), axis=1)
    high = lax.reduce_precision(weight, exponent_bits=8, mantissa_bits=7)
    half = -(-2 * slot_count // LANE) * LANE // 2
    pad = jnp.zeros((tokens.shape[0], half - slot_count), jnp.bfloat16)
    sent = jnp.concatenate(
        [tokens, high.astype(jnp.bfloat16), pad, (weight - high).astype(jnp.bfloat16), pad], axis=1
    )
    rows = lax.all_gather(sent, "exp", axis=0, tiled=True)
    full_in = lax.all_gather(w_in, "grp", axis=1, tiled=True)
    full_out = lax.all_gather(w_out, "grp", axis=1, tiled=True)

    same_expert = new_plan[:, None] == old_plan[None, :]
    source = jnp.min(jnp.where(same_expert, slot_index[None, :], slot_count), axis=1)
    (new_moments_in,) = reshuffle((moments_in,), source, devices)
    new_w_in, new_w_out, new_moments_out = reshuffle((w_in, w_out, moments_out), source, devices)

    first = (lax.axis_index("exp") * per_device).astype(jnp.int32).reshape(1)
    held = rows.reshape(devices, -1, rows.shape[1])

    def finished(part):
        size = part.shape[1]
        partial = experts(part.reshape(devices * size, -1), full_in, full_out, first)
        return lax.psum_scatter(partial, "exp", scatter_dimension=0, tiled=True)

    parts = -(-rows.shape[0] * tokens.shape[1] * 4 // PARTIAL_BYTES)
    if parts == 1:
        mixed = finished(held)
    else:
        size = held.shape[1] // parts
        mixed = lax.map(
            lambda p: finished(lax.dynamic_slice_in_dim(held, p * size, size, axis=1)),
            jnp.arange(parts, dtype=jnp.int32),
        ).reshape(tokens.shape)
    return (mixed.astype(jnp.bfloat16), new_w_in, new_w_out, new_moments_in, new_moments_out)


def solution(mesh):
    return jax.shard_map(
        on_device,
        mesh=mesh,
        in_specs=(
            P(("grp", "exp"), None),
            P("exp", "grp", None),
            P("exp", "grp", None),
            P("exp", None, "grp", None),
            P("exp", None, "grp", None),
            P(("grp", "exp"), None),
            P(("grp", "exp"), None),
            P(),
            P(),
        ),
        out_specs=(
            P(("grp", "exp"), None),
            P("exp", "grp", None),
            P("exp", "grp", None),
            P("exp", None, "grp", None),
            P("exp", None, "grp", None),
        ),
        check_vma=False,
    )
```

time: 629 us -> 436 us (0.69)
  the two profiles are of different devices: /device:TPU:11 before, /device:TPU:21 now
where the time goes in v1:
time: 436 us; the launch traced here: 435 us
  waiting for transfers between devices  347 us (80%)
  local copies, waits for them, and re-layouts  28.3 us (6%)
  starting transfers between devices  24.2 us (6%)
  Pallas kernels  16.8 us (4%)
  between operations  13.9 us (3%)
  other arithmetic  5.25 us (1%)
    all_to_all x2, waiting for transfers between devices, reshuffle(): lax.all_to_all(packed, 'exp', split_axis=0, concat_axis=0, tiled=True)  174 us
    all_to_all x2, waiting for transfers between devices, reshuffle(): lax.all_to_all(picked, 'exp', split_axis=0, concat_axis=0, tiled=True)  172 us
    pallas_call x1, Pallas kernels, experts(): pl.pallas_call(expert_kernel, grid=(rows // block,), in_specs=[pl.BlockSp...  16.8 us
    all_to_all x2, starting transfers between devices, reshuffle(): lax.all_to_all(picked, 'exp', split_axis=0, concat_axis=0, tiled=True)  12.3 us
    all_to_all x2, starting transfers between devices, reshuffle(): lax.all_to_all(packed, 'exp', split_axis=0, concat_axis=0, tiled=True)  11.8 us
  transfers between devices with their start and end apart: 8, of which 4 were waited for; matrix products, arithmetic and copies ran while one was open for 6% of the time, Pallas kernels for 4%

profile of v1, /device:TPU:21, one launch (start us, length us, event | category | flops | bytes accessed | tf_op | source)
XLA Modules:
  0.0 435.5 jit_solution(9372435706376006129)
XLA Ops:
  7.2 0.0 all-gather.8.cloned.1.call-start
  7.2 0.7 all-gather.8.cloned.1.call-update
  7.9 3.9 copy.41
  11.8 0.0 copy-start.6
  11.8 6.6 %all-to-all-start.2 = ((bf16[16,2,48,8,128]{4,3,2,1,0:T(8,128)(2,1)}), bf16[16,2,48,8,128]{4,3,2,1,0:T(8,128)(2,1)S(1)}, u32[]{:S(2)}, u32[]{:S(2)}) async-start(bf16[16,2,48,8,128]{4,3,2,1,0:T(8,128)(2,1)} %copy.41), calls=%async_computation.3 | async-start | bytes 6291456 | tf_op jit(solution)/shard_map/all_to_all | solution.py:36
  18.4 0.0 all-gather.6.cloned.1.call-start
  18.5 0.7 all-gather.6.cloned.1.call-update
  19.2 0.0 all-gather.4.cloned.1.call-start
  19.2 0.0 copy-done.6
  19.2 0.2 fusion.1
  19.4 0.0 copy-done.4
  19.5 0.0 copy-done.5
  19.5 0.1 select_reduce_fusion
  19.6 0.1 copy.37
  19.7 0.1 copy.36
  19.8 0.6 subtract_convert_fusion
  20.4 0.0 copy-done.3
  20.4 1.6 concatenate.6
  22.0 0.0 all-gather.4.cloned.1.call-update
  22.1 2.3 pad_maximum_fusion
  24.4 2.3 copy.39
  26.7 61.4 %all-to-all-done.2 = bf16[16,2,48,8,128]{4,3,2,1,0:T(8,128)(2,1)S(1)} async-done(((bf16[16,2,48,8,128]{4,3,2,1,0:T(8,128)(2,1)}), bf16[16,2,48,8,128]{4,3,2,1,0:T(8,128)(2,1)S(1)}, u32[]{:S(2)}, u32[]{:S(2)}) %all-to-all-start.2) | async-done | bytes 3145760 | tf_op jit(solution)/shard_map/all_to_all | solution.py:36
  88.0 5.2 %all-to-all-start = ((bf16[16,2,60,8,128]{4,3,2,1,0:T(8,128)(2,1)}), bf16[16,2,60,8,128]{4,3,2,1,0:T(8,128)(2,1)}, u32[]{:S(2)}, u32[]{:S(2)}) async-start(bf16[16,2,60,8,128]{4,3,2,1,0:T(8,128)(2,1)} %copy.39), calls=%async_computation.1 | async-start | bytes 7864320 | tf_op jit(solution)/shard_map/all_to_all | solution.py:36
  93.2 0.0 copy-done.7
  93.2 0.0 copy-done.8
  93.2 0.2 select_reduce_fusion.1
  93.4 2.6 gather_fusion.1
  96.0 112.1 %all-to-all-done = bf16[16,2,60,8,128]{4,3,2,1,0:T(8,128)(2,1)} async-done(((bf16[16,2,60,8,128]{4,3,2,1,0:T(8,128)(2,1)}), bf16[16,2,60,8,128]{4,3,2,1,0:T(8,128)(2,1)}, u32[]{:S(2)}, u32[]{:S(2)}) %all-to-all-start) | async-done | bytes 3932192 | tf_op jit(solution)/shard_map/all_to_all | solution.py:36
  208.2 5.2 %all-to-all-start.3 = ((bf16[16,2,48,8,128]{4,3,2,1,0:T(8,128)(2,1)}), bf16[16,2,48,8,128]{4,3,2,1,0:T(8,128)(2,1)S(1)}, u32[]{:S(2)}, u32[]{:S(2)}) async-start(bf16[16,2,48,8,128]{4,3,2,1,0:T(8,128)(2,1)} %bitcast.59), calls=%async_computation.4 | async-start | bytes 6291456 | tf_op jit(solution)/shard_map/all_to_all | solution.py:40
  213.4 0.0 reduce-scatter.2.cloned.1.call-start
  213.5 0.0 all-gather.8.cloned.1.call-done.w_out_ref
  213.5 0.0 all-gather.6.cloned.1.call-done.w_in_ref
  213.5 0.0 all-gather.4.cloned.1.call-done.x_ref
  213.5 0.0 copy-start
  213.6 2.3 copy-done
  215.9 1.9 copy-done.1
  217.8 1.4 copy-done.2
  219.2 16.8 %shard_map.128 = f32[2048,1024]{1,0:T(8,128)} custom-call(s32[1]{0:T(128)} %bitcast.first_ref, bf16[2048,1152]{1,0:T(8,128)(2,1)S(1)} %copy-done, bf16[2,1024,768]{2,1,0:T(8,128)(2,1)S(1)} %copy-done.1, bf16[2,384,1024]{2,1,0:T(8,128)(2,1)S(1)} %copy-done.2), custom_call_target="tpu_custom_call" | custom-call | flops 9663676416 | bytes 17825792 | tf_op jit(solution)/shard_map/pallas_call | solution.py:74
  236.0 0.0 reduce-scatter.2.cloned.1.call-update
  236.0 5.0 %gather_fusion = bf16[32,60,8,128]{3,2,1,0:T(8,128)(2,1)} fusion(bf16[32,60,8,128]{3,2,1,0:T(8,128)(2,1)} %bitcast.12, s32[1024]{0:T(1024)S(1)} %pad_clamp_fusion), kind=kCustom, calls=%fused_computation | custom fusion | bytes 7864448 | tf_op jit(solution)/shard_map/jit(_take)/gather | solution.py:38
  241.0 69.9 %all-to-all-done.3 = bf16[16,2,48,8,128]{4,3,2,1,0:T(8,128)(2,1)S(1)} async-done(((bf16[16,2,48,8,128]{4,3,2,1,0:T(8,128)(2,1)}), bf16[16,2,48,8,128]{4,3,2,1,0:T(8,128)(2,1)S(1)}, u32[]{:S(2)}, u32[]{:S(2)}) %all-to-all-start.3) | async-done | bytes 3145760 | tf_op jit(solution)/shard_map/all_to_all | solution.py:40
  311.0 7.0 %all-to-all-start.1 = ((bf16[16,2,60,8,128]{4,3,2,1,0:T(8,128)(2,1)}), bf16[16,2,60,8,128]{4,3,2,1,0:T(8,128)(2,1)}, u32[]{:S(2)}, u32[]{:S(2)}) async-start(bf16[16,2,60,8,128]{4,3,2,1,0:T(8,128)(2,1)} %bitcast.55), calls=%async_computation.2 | async-start | bytes 7864320 | tf_op jit(solution)/shard_map/all_to_all | solution.py:40
  318.0 1.9 copy.42
  319.9 102.1 %all-to-all-done.1 = bf16[16,2,60,8,128]{4,3,2,1,0:T(8,128)(2,1)} async-done(((bf16[16,2,60,8,128]{4,3,2,1,0:T(8,128)(2,1)}), bf16[16,2,60,8,128]{4,3,2,1,0:T(8,128)(2,1)}, u32[]{:S(2)}, u32[]{:S(2)}) %all-to-all-start.1) | async-done | bytes 3932192 | tf_op jit(solution)/shard_map/all_to_all | solution.py:40
  422.0 2.4 copy.40
  424.4 0.9 slice.17
  425.3 1.9 fusion.2
  427.2 1.8 convert_element_type.11
  (14 shorter events, 0.1 us)
Async XLA Ops:
  7.2 206.3 %all-gather.8.cloned.1.call-start = ((), (), s32[]{:S(2)}) async-start(), calls=%async_computation.7 | async-start | bytes 2359296 | tf_op jit(solution)/shard_map/all_gather | solution.py:115
  11.8 7.4 %copy-start.6 = (s32[32]{0:T(128)S(1)}, s32[32]{0:T(128)}, u32[]{:S(2)}) copy-start(s32[32]{0:T(128)} %param.16) | copy-start | bytes 388
  11.8 7.6 %copy-start.4 = (f32[128,8]{0,1:T(8,128)S(1)}, f32[128,8]{0,1:T(8,128)}, u32[]{:S(2)}) copy-start(f32[128,8]{0,1:T(8,128)} %param.15) | copy-start | bytes 12292
  11.8 7.7 %copy-start.5 = (s32[128,8]{0,1:T(8,128)S(1)}, s32[128,8]{0,1:T(8,128)}, u32[]{:S(2)}) copy-start(s32[128,8]{0,1:T(8,128)} %param.14) | copy-start | bytes 12292
  11.8 8.6 %copy-start.3 = (bf16[128,1024]{1,0:T(8,128)(2,1)S(1)}, bf16[128,1024]{1,0:T(8,128)(2,1)}, u32[]{:S(2)}) copy-start(bf16[128,1024]{1,0:T(8,128)(2,1)} %param.9) | copy-start | bytes 786436
  11.8 76.2 %all-to-all-start.2 = ((bf16[16,2,48,8,128]{4,3,2,1,0:T(8,128)(2,1)}), bf16[16,2,48,8,128]{4,3,2,1,0:T(8,128)(2,1)S(1)}, u32[]{:S(2)}, u32[]{:S(2)}) async-start(bf16[16,2,48,8,128]{4,3,2,1,0:T(8,128)(2,1)} %copy.41), calls=%async_computation.3 | async-start | bytes 6291456 | tf_op jit(solution)/shard_map/all_to_all | solution.py:36
  18.4 195.1 %all-gather.6.cloned.1.call-start = ((), (), s32[]{:S(2)}) async-start(), calls=%async_computation.6 | async-start | bytes 4718592 | tf_op jit(solution)/shard_map/all_gather | solution.py:114
  19.2 194.4 %all-gather.4.cloned.1.call-start = ((), (), s32[]{:S(2)}) async-start(), calls=%async_computation.5 | async-start | bytes 5013504 | tf_op jit(solution)/shard_map/all_gather | solution.py:113
  26.7 66.6 %copy-start.7 = (s32[32]{0:T(128)S(1)}, s32[32]{0:T(128)}, u32[]{:S(2)}) copy-start(s32[32]{0:T(128)} %param.16) | copy-start | bytes 388
  26.7 66.6 %copy-start.8 = (s32[32]{0:T(128)S(1)}, s32[32]{0:T(128)}, u32[]{:S(2)}) copy-start(s32[32]{0:T(128)} %param.17) | copy-start | bytes 388
  88.0 120.2 %all-to-all-start = ((bf16[16,2,60,8,128]{4,3,2,1,0:T(8,128)(2,1)}), bf16[16,2,60,8,128]{4,3,2,1,0:T(8,128)(2,1)}, u32[]{:S(2)}, u32[]{:S(2)}) async-start(bf16[16,2,60,8,128]{4,3,2,1,0:T(8,128)(2,1)} %copy.39), calls=%async_computation.1 | async-start | bytes 7864320 | tf_op jit(solution)/shard_map/all_to_all | solution.py:36
  208.2 102.8 %all-to-all-start.3 = ((bf16[16,2,48,8,128]{4,3,2,1,0:T(8,128)(2,1)}), bf16[16,2,48,8,128]{4,3,2,1,0:T(8,128)(2,1)S(1)}, u32[]{:S(2)}, u32[]{:S(2)}) async-start(bf16[16,2,48,8,128]{4,3,2,1,0:T(8,128)(2,1)} %bitcast.59), calls=%async_computation.4 | async-start | bytes 6291456 | tf_op jit(solution)/shard_map/all_to_all | solution.py:40
  213.4 213.7 %reduce-scatter.2.cloned.1.call-start = ((), (), s32[]{:S(2)}) async-start(), calls=%async_computation.8 | async-start | bytes 8912896 | tf_op jit(solution)/shard_map/reduce_scatter | solution.py:128
  213.5 2.3 copy-start
  215.9 1.9 copy-start.1
  217.8 1.4 copy-start.2
  311.0 111.0 %all-to-all-start.1 = ((bf16[16,2,60,8,128]{4,3,2,1,0:T(8,128)(2,1)}), bf16[16,2,60,8,128]{4,3,2,1,0:T(8,128)(2,1)}, u32[]{:S(2)}, u32[]{:S(2)}) async-start(bf16[16,2,60,8,128]{4,3,2,1,0:T(8,128)(2,1)} %bitcast.55), calls=%async_computation.2 | async-start | bytes 7864320 | tf_op jit(solution)/shard_map/all_to_all | solution.py:40
Sparse Core Ops, SparseCore 0:
  9.5 27.3 all-gather.7
  38.4 44.9 all-gather.5
  86.3 105.4 all-gather.3
  236.1 163.9 reduce-scatter.1
